TPU v7x, 128 devices: a whole 4x4x4 slice. The times are simulated.
128 devices in a mesh: tm: 8 (over y, core), expert: 16 (over z, x).
Axes of the slice: x: 4, y: 4, z: 4, core: 2. Of those that a mesh axis runs over, the one named last changes fastest.
Arguments:
- queries: bfloat16 [16384, 2048], P(('tm', 'expert')), may hold values from -6 to 6
- keys: bfloat16 [16384, 2048], P(('tm', 'expert')), may hold values from -6 to 6
- values: bfloat16 [16384, 2048], P(('tm', 'expert')), may hold values from -6 to 6
- out_grad: bfloat16 [16384, 2048], P(('tm', 'expert')), may hold values from -6 to 6
- expert_ids: int32 [16384, 2], P(('tm', 'expert')), may hold values from 0 to 31, all different within a row
- combine_gates: float32 [16384, 2], P(('tm', 'expert')), may hold values from 0.2 to 1
- gate_weight: bfloat16 [128, 2048, 512], P(('tm', 'expert')), may hold values from -0.125 to 0.125
- up_weight: bfloat16 [128, 2048, 512], P(('tm', 'expert')), may hold values from -0.125 to 0.125
- down_weight: bfloat16 [128, 512, 2048], P(('tm', 'expert')), may hold values from -0.125 to 0.125
Outputs:
- query_grad: bfloat16 [16384, 2048], P(('tm', 'expert'))
- key_grad: bfloat16 [16384, 2048], P(('tm', 'expert'))
- value_grad: bfloat16 [16384, 2048], P(('tm', 'expert'))
- gate_weight_grad: float32 [128, 2048, 512], P(('tm', 'expert'))
- up_weight_grad: float32 [128, 2048, 512], P(('tm', 'expert'))
- down_weight_grad: float32 [128, 512, 2048], P(('tm', 'expert'))
Inputs may be any that keep to these rules, and one draw needn't show every extreme that they name: `expert_ids`: the two experts of a token differ.
All inputs are finite; a program needn't handle non-finite values.
Results may differ from a plain program's by a relative error of at most 0.017.
Values may be sent and summed in bfloat16 or wider, within the bound.
A program may use at most 192 MiB of HBM per device.

v0:
```python
import jax
import jax.numpy as jnp
from jax import lax
from jax.sharding import PartitionSpec as P

HEADS = 16
HEAD_DIM = 128
SLICES = 4
epsilon = 1e-06
highest = lax.Precision.HIGHEST


def side_by_side(arrays, axis, split_dim, concat_dim, along):
    widths = [a.shape[along] for a in arrays]
    both = jnp.concatenate(arrays, axis=along)
    whole = lax.all_to_all(both, axis, split_axis=split_dim, concat_axis=concat_dim, tiled=True)
    return tuple(jnp.split(whole, [sum(widths[:k]) for k in range(1, len(widths))], axis=along))


def slot_places(routes, capacity, experts):
    flat_ids = routes.reshape(-1)
    onehot = (flat_ids[:, None] == jnp.arange(experts, dtype=jnp.int32)[None, :]).astype(jnp.int32)
    earlier = jnp.cumsum(onehot, axis=0) - onehot
    position = jnp.sum(earlier * onehot, axis=1)
    return jnp.where(position < capacity, flat_ids * capacity + position, experts * capacity)


def expert_slice(rows, grad_rows, gate_part, up_part, down_part):
    gate = jnp.dot(rows, gate_part, preferred_element_type=jnp.float32)
    upper = jnp.dot(rows, up_part, preferred_element_type=jnp.float32)
    sigma = jax.nn.sigmoid(gate)
    act = (gate * sigma * upper).astype(jnp.bfloat16)
    act_grad = jnp.dot(grad_rows, down_part.T, preferred_element_type=jnp.float32)
    down_grad = jnp.dot(act.T, grad_rows, preferred_element_type=jnp.float32)
    gate_grad = (act_grad * upper * sigma * (1.0 + gate * (1.0 - sigma))).astype(jnp.bfloat16)
    up_grad = (act_grad * gate * sigma).astype(jnp.bfloat16)
    gate_wgrad = jnp.dot(rows.T, gate_grad, preferred_element_type=jnp.float32)
    up_wgrad = jnp.dot(rows.T, up_grad, preferred_element_type=jnp.float32)
    partial_sum = jnp.dot(gate_grad, gate_part.T, preferred_element_type=jnp.float32)
    partial_sum = partial_sum + jnp.dot(up_grad, up_part.T, preferred_element_type=jnp.float32)
    return (partial_sum.astype(jnp.bfloat16), gate_wgrad, up_wgrad, down_grad)


def body(
    queries, keys, values, out_grad, expert_ids, combine_gates, gate_weight, up_weight, down_weight
):
    tok_rows = queries.shape[0]
    width = queries.shape[1]
    time_count = lax.axis_size("tm")
    group_count = lax.axis_size("expert")
    devices = time_count * group_count
    experts = devices // SLICES
    capacity = SLICES * max(1, 3 * tok_rows // (experts * SLICES))
    shape3 = (tok_rows, HEADS, HEAD_DIM)
    query_f = queries.astype(jnp.float32).reshape(shape3)
    key_f = keys.astype(jnp.float32).reshape(shape3)
    value_f = values.astype(jnp.float32).reshape(shape3)
    local = jnp.einsum("tha,thb->hab", key_f, value_f, precision=highest)
    everyone = lax.all_gather(local[None], "tm", axis=0, tiled=True)
    mine = lax.axis_index("tm")
    picks = (jnp.arange(everyone.shape[0], dtype=jnp.int32) <= mine).astype(jnp.float32)
    inclusive = jnp.einsum("c,chab->hab", picks, everyone, precision=highest)
    states = lax.psum(inclusive, "expert")
    mixed = jnp.einsum("tha,hab->thb", query_f, states, precision=highest)
    scale = lax.rsqrt(jnp.mean(mixed * mixed, axis=-1, keepdims=True) + epsilon)
    normed = mixed * scale
    hidden = normed.astype(jnp.bfloat16).reshape(tok_rows, width)
    places = slot_places(expert_ids, capacity, experts)
    rows_h = jnp.repeat(hidden, 2, axis=0)
    grad_f = out_grad.astype(jnp.float32)
    rows_g = (jnp.repeat(grad_f, 2, axis=0) * combine_gates.reshape(-1, 1)).astype(jnp.bfloat16)
    buffer_h = (
        jnp.zeros((experts * capacity, width), jnp.bfloat16).at[places].set(rows_h, mode="drop")
    )
    buffer_g = (
        jnp.zeros((experts * capacity, width), jnp.bfloat16).at[places].set(rows_g, mode="drop")
    )
    send_h = jnp.repeat(buffer_h.reshape(experts, capacity, width), SLICES, axis=0)
    send_g = jnp.repeat(buffer_g.reshape(experts, capacity, width), SLICES, axis=0)
    got_h, got_g = side_by_side((send_h, send_g), ("tm", "expert"), 0, 0, 1)
    got_h = got_h.reshape(1, devices, capacity, width)
    got_g = got_g.reshape(1, devices, capacity, width)
    rows = got_h.reshape(-1, width)
    grad_rows = got_g.reshape(-1, width)
    partial_sum, gate_wgrad, up_wgrad, down_grad = expert_slice(
        rows, grad_rows, gate_weight[0], up_weight[0], down_weight[0]
    )
    payload = partial_sum.astype(jnp.float32).reshape(devices, capacity, width)
    returned = lax.all_to_all(
        payload.astype(jnp.bfloat16), ("tm", "expert"), split_axis=0, concat_axis=0, tiled=True
    ).astype(payload.dtype)
    summed = jnp.sum(returned.reshape(experts, SLICES, capacity, width), axis=1)
    per_choice = jnp.take(
        summed.reshape(experts * capacity, width), places, axis=0, mode="fill", fill_value=0.0
    )
    moe_grad = jnp.sum(per_choice.reshape(tok_rows, 2, width), axis=1)
    hidden_grad = (grad_f + moe_grad).reshape(shape3)
    norm_grad = scale * (
        hidden_grad - normed * jnp.mean(hidden_grad * normed, axis=-1, keepdims=True)
    )
    query_grad = jnp.einsum("thb,hab->tha", norm_grad, states, precision=highest)
    local_back = jnp.einsum("tha,thb->hab", query_f, norm_grad, precision=highest)
    every_back = lax.all_gather(
        local_back[None].astype(jnp.bfloat16), "tm", axis=0, tiled=True
    ).astype(jnp.float32)
    mine_back = lax.axis_index("tm")
    picks_back = (jnp.arange(every_back.shape[0], dtype=jnp.int32) >= mine_back).astype(jnp.float32)
    inclusive_back = jnp.einsum("c,chab->hab", picks_back, every_back, precision=highest)
    back_states = lax.psum(inclusive_back.astype(jnp.bfloat16), "expert").astype(jnp.float32)
    key_grad = jnp.einsum("thb,hab->tha", value_f, back_states, precision=highest)
    value_grad = jnp.einsum("tha,hab->thb", key_f, back_states, precision=highest)
    return (
        query_grad.reshape(tok_rows, width).astype(jnp.bfloat16),
        key_grad.reshape(tok_rows, width).astype(jnp.bfloat16),
        value_grad.reshape(tok_rows, width).astype(jnp.bfloat16),
        gate_wgrad[None],
        up_wgrad[None],
        down_grad[None],
    )


def solution(mesh):
    placed = (
        P(("tm", "expert"), None),
        P(("tm", "expert"), None),
        P(("tm", "expert"), None),
        P(("tm", "expert"), None),
        P(("tm", "expert"), None),
        P(("tm", "expert"), None),
        P(("tm", "expert"), None, None),
        P(("tm", "expert"), None, None),
        P(("tm", "expert"), None, None),
    )
    return jax.shard_map(
        body,
        mesh=mesh,
        in_specs=placed,
        out_specs=(
            P(("tm", "expert"), None),
            P(("tm", "expert"), None),
            P(("tm", "expert"), None),
            P(("tm", "expert"), None, None),
            P(("tm", "expert"), None, None),
            P(("tm", "expert"), None, None),
        ),
        check_vma=False,
    )
```

profile of v0, /device:TPU:0, one launch (start us, length us, event | category | flops | bytes accessed | tf_op | source)
XLA Modules:
  0.0 693.4 jit_solution(2359564202389222377)
XLA Ops:
  7.2 2.7 fusion.23
  10.0 52.6 %all-gather.5.cloned.1.call-done = f32[128,128,128]{2,1,0:T(8,128)} async-done(((f32[16,128,128]{2,1,0:T(8,128)}), f32[128,128,128]{2,1,0:T(8,128)}) %all-gather.5.cloned.1.call-update) | async-done | bytes 8388624 | tf_op jit(solution)/shard_map/all_gather | solution.py:59
  62.5 11.8 %fusion = f32[1,16,128,128]{3,0,2,1:T(1,128)S(1)} fusion(f32[8,16,128,128]{3,2,1,0:T(8,128)} %bitcast.136, s32[]{:T(128)S(6)} %axis_index.19), kind=kOutput, calls=%fused_computation.6 | convolution fusion | flops 25165832 | bytes 9437188 | tf_op jit(solution)/shard_map/c,chab->hab/dot_general | solution.py:62
  74.4 2.1 copy.71
  76.5 0.1 copy.52
  76.7 0.1 eq.29
  76.8 0.1 eq.25
  77.0 0.6 reduce-window.6
  77.5 0.2 slice_reduce_fusion
  77.8 0.1 mul.85
  77.9 0.1 copy.57
  78.1 0.1 mul.87
  78.2 3.4 broadcast_in_dim.52
  81.6 3.6 reshape.151
  85.4 4.5 scatter_custom_fusion.1
  89.9 3.6 reshape.152
  93.5 70.4 %all-reduce.3.cloned.1.call-done = f32[16,128,128]{1,2,0:T(8,128)} async-done(((f32[16,128,128]{1,2,0:T(8,128)}), f32[16,128,128]{1,2,0:T(8,128)}) %all-reduce.3.cloned.1.call-update) | async-done | bytes 1048592 | tf_op jit(solution)/shard_map/psum | solution.py:63
  164.0 2.4 multiply_reduce_fusion.1
  166.4 1.0 copy-done.2
  167.4 0.1 multiply_convert_fusion.6
  167.5 1.0 copy.56
  168.6 1.7 broadcast_in_dim.50
  170.2 1.2 reshape.172
  171.5 4.1 scatter_custom_fusion
  175.6 3.6 reshape.149
  179.2 6.1 broadcast_in_dim.53
  185.2 4.3 broadcast_in_dim.51
  189.5 9.2 %pad_maximum_fusion = bf16[128,24,2048]{2,1,0:T(8,128)(2,1)S(1)} fusion(bf16[128,12,2048]{2,1,0:T(8,128)(2,1)} %bitcast.132, bf16[128,12,2048]{2,1,0:T(8,128)(2,1)} %bitcast.133), kind=kLoop, calls=%fused_computation.4 | loop fusion | flops 25165824 | bytes 25165824 | tf_op jit(solution)/shard_map/concatenate | solution.py:15
  198.7 149.2 %all_to_all.10 = bf16[128,24,2048]{2,1,0:T(8,128)(2,1)S(1)} all-to-all(bf16[128,24,2048]{2,1,0:T(8,128)(2,1)S(1)} %pad_maximum_fusion), channel_id=1, replica_groups=mesh['tm'=8,'expert'=16] {'tm','expert'}, dimensions={0} | all-to-all | bytes 25165824 | tf_op jit(solution)/shard_map/all_to_all | solution.py:16
  347.9 7.1 %fusion.46 = (bf16[128,12,2048]{2,1,0:T(8,128)(2,1)}, bf16[128,12,2048]{2,1,0:T(8,128)(2,1)}) fusion(bf16[128,24,2048]{2,1,0:T(8,128)(2,1)S(1)} %all_to_all.10), kind=kLoop, calls=%fused_computation.84 | loop fusion | bytes 25165824 | tf_op jit(solution)/shard_map/split | solution.py:17
  355.0 10.7 %reshape_reshape.6 = bf16[1536,2048]{1,0:T(8,128)(2,1)} reshape(bf16[128,12,2048]{2,1,0:T(8,128)(2,1)} %get-tuple-element.24) | data formatting | bytes 12582912 | tf_op jit(solution)/shard_map/reshape;reshape | solution.py:84
  365.7 10.7 %reshape_reshape.7 = bf16[1536,2048]{1,0:T(8,128)(2,1)} reshape(bf16[128,12,2048]{2,1,0:T(8,128)(2,1)} %get-tuple-element.25) | data formatting | bytes 12582912 | tf_op jit(solution)/shard_map/reshape;reshape | solution.py:83
  376.4 6.0 fusion.6
  382.4 3.4 fusion.9
  385.9 4.8 multiply_convert_fusion.1
  390.8 6.5 fusion.4
  397.3 8.5 %add_convert_fusion = bf16[1536,2048]{1,0:T(8,128)(2,1)} fusion(f32[1536,2048]{1,0:T(8,128)} %fusion.4, bf16[1536,512]{1,0:T(8,128)(2,1)S(1)} %get-tuple-element.26, bf16[1,2048,512]{2,1,0:T(8,128)(2,1)S(1)} %copy-done.13), kind=kOutput, calls=%fused_computation.5 | convolution fusion | flops 3227516928 | bytes 22544384 | tf_op jit(solution)/shard_map/dot_general | solution.py:40
  405.8 10.6 %convert_element_type.88 = bf16[128,12,2048]{2,1,0:T(8,128)(2,1)} reshape(bf16[1536,2048]{1,0:T(8,128)(2,1)} %add_convert_fusion) | data formatting | bytes 12582912 | tf_op jit(solution)/shard_map/convert_element_type | solution.py:90
  416.4 6.9 all-to-all-start.1
  423.4 0.1 reduce_sum.51
  423.6 99.8 %all-to-all-done.1 = bf16[128,12,2048]{2,1,0:T(8,128)(2,1)} async-done(((bf16[128,12,2048]{2,1,0:T(8,128)(2,1)}), bf16[128,12,2048]{2,1,0:T(8,128)(2,1)}, u32[]{:S(2)}, u32[]{:S(2)}) %all-to-all-start.1) | async-done | bytes 6291488 | tf_op jit(solution)/shard_map/all_to_all | solution.py:89
  523.4 7.8 %convert_reduce_fusion = f32[32,12,2048]{2,1,0:T(8,128)} fusion(bf16[128,12,2048]{2,1,0:T(8,128)(2,1)} %all-to-all-done.1), kind=kLoop, calls=%fused_computation.3 | loop fusion | flops 5505024 | bytes 9437184 | tf_op jit(solution)/shard_map/reduce_sum | solution.py:92
  531.2 3.0 reshape.156
  534.2 2.7 gather_fusion
  536.9 2.5 gather.7
  539.4 4.5 select_reduce_fusion
  544.0 0.3 copy.58
  544.4 0.8 copy-done.3
  545.1 0.2 multiply_reduce_fusion
  545.3 1.8 fusion.14
  547.1 1.0 copy.62
  548.2 8.9 %convolution_bitcast_fusion.1 = f32[1,2048,512]{2,1,0:T(8,128)} fusion(bf16[1536,2048]{1,0:T(8,128)(2,1)} %reshape_reshape.7, bf16[1536,512]{1,0:T(8,128)(2,1)} %copy-done.14), kind=kOutput, calls=%fused_computation.11 | convolution fusion | flops 3221225472 | bytes 12058624 | tf_op jit(solution)/shard_map/dot_general | solution.py:38
  557.1 8.3 %convolution_bitcast_fusion = f32[1,512,2048]{2,1,0:T(8,128)} fusion(bf16[1536,2048]{1,0:T(8,128)(2,1)} %reshape_reshape.6, f32[1536,512]{1,0:T(8,128)S(1)} %copy-done.19, f32[1536,512]{1,0:T(8,128)S(1)} %copy-done.17), kind=kOutput, calls=%fused_computation.10 | convolution fusion | flops 3225944064 | bytes 16777216 | tf_op jit(solution)/shard_map/dot_general | solution.py:34
  565.4 24.5 %all-gather.7.cloned.1.call-done = bf16[128,128,128]{2,1,0:T(8,128)(2,1)} async-done(((bf16[16,128,128]{2,1,0:T(8,128)(2,1)}), bf16[128,128,128]{2,1,0:T(8,128)(2,1)}) %all-gather.7.cloned.1.call-update) | async-done | bytes 4194320 | tf_op jit(solution)/shard_map/all_gather | solution.py:103
  589.9 4.9 fusion.2
  594.9 0.9 convert_element_type.95
  595.8 8.8 %convolution_bitcast_fusion.2 = f32[1,2048,512]{2,1,0:T(8,128)} fusion(bf16[1536,2048]{1,0:T(8,128)(2,1)} %reshape_reshape.7, bf16[1536,512]{1,0:T(8,128)(2,1)} %copy-done.15), kind=kOutput, calls=%fused_computation.12 | convolution fusion | flops 3221225472 | bytes 12058624 | tf_op jit(solution)/shard_map/dot_general | solution.py:37
  604.6 2.0 convolution_convert_fusion.3
  606.6 1.0 copy.66
  607.6 73.6 %all-reduce.5.cloned.1.call-done = bf16[16,128,128]{2,1,0:T(8,128)(2,1)} async-done(((bf16[16,128,128]{2,1,0:T(8,128)(2,1)}), bf16[16,128,128]{2,1,0:T(8,128)(2,1)}) %all-reduce.5.cloned.1.call-update) | async-done | bytes 524304 | tf_op jit(solution)/shard_map/psum | solution.py:109
  681.2 1.5 convolution_convert_fusion.1
  682.7 1.0 copy.67
  683.7 1.7 convolution_convert_fusion
  685.4 1.0 copy.68
  (62 shorter events, 0.7 us)
Async XLA Ops:
  7.2 369.2 %copy-start = (bf16[1,2048,512]{2,1,0:T(8,128)(2,1)S(1)}, bf16[1,2048,512]{2,1,0:T(8,128)(2,1)}, u32[]{:S(2)}) copy-start(bf16[1,2048,512]{2,1,0:T(8,128)(2,1)} %param.15) | copy-start | bytes 6291460
  7.2 55.4 %all-gather.5.cloned.1.call-start = ((), (), s32[]{:S(2)}) async-start(), calls=%async_computation.4 | async-start | bytes 9437184 | tf_op jit(solution)/shard_map/all_gather | solution.py:59
  9.9 154.0 %all-reduce.3.cloned.1.call-start = ((), (), s32[]{:S(2)}) async-start(), calls=%async_computation.2 | async-start | bytes 2097152 | tf_op jit(solution)/shard_map/psum | solution.py:63
  74.4 2.1 copy-start.10
  74.4 3.5 copy-start.11
  85.4 78.6 %copy-start.8 = (bf16[128,2048]{1,0:T(8,128)(2,1)S(1)}, bf16[128,2048]{1,0:T(8,128)(2,1)}, u32[]{:S(2)}) copy-start(bf16[128,2048]{1,0:T(8,128)(2,1)} %param.9) | copy-start | bytes 1572868
  166.4 1.0 copy-start.2
  179.2 6.1 copy-start.4
  376.4 6.0 copy-start.5
  376.4 6.0 copy-start.13
  376.4 9.5 %slice-start = ((s8[6291456]{0:T(1024)(128)(4,1)}), s8[4194304]{0:T(1024)(128)(4,1)S(1)}, s32[]{:S(2)}) async-start(s8[6291456]{0:T(1024)(128)(4,1)} %bitcast.137), calls=%async_computation.6 | async-start | bytes 8388608
  382.4 3.5 copy-start.16
  382.4 3.5 slice-start.1
  382.4 3.5 copy-start.12
  385.9 4.9 copy-start.18
  390.8 6.5 copy-start.15
  390.8 6.5 copy-start.14
  416.4 106.9 %all-to-all-start.1 = ((bf16[128,12,2048]{2,1,0:T(8,128)(2,1)}), bf16[128,12,2048]{2,1,0:T(8,128)(2,1)}, u32[]{:S(2)}, u32[]{:S(2)}) async-start(bf16[128,12,2048]{2,1,0:T(8,128)(2,1)} %convert_element_type.88), calls=%async_computation.1 | async-start | bytes 16777216 | tf_op jit(solution)/shard_map/all_to_all | solution.py:89
  423.3 166.6 %all-gather.7.cloned.1.call-start = ((), (), s32[]{:S(2)}) async-start(), calls=%async_computation.5 | async-start | bytes 4718592 | tf_op jit(solution)/shard_map/all_gather | solution.py:103
  539.4 4.5 copy-start.7
  543.9 1.2 copy-start.3
  548.2 133.0 %all-reduce.5.cloned.1.call-start = ((), (), s32[]{:S(2)}) async-start(), calls=%async_computation.3 | async-start | bytes 1048576 | tf_op jit(solution)/shard_map/psum | solution.py:109
  548.2 8.9 %copy-start.17 = (f32[1536,512]{1,0:T(8,128)S(1)}, f32[1536,512]{1,0:T(8,128)}, u32[]{:S(2)}) copy-start(f32[1536,512]{1,0:T(8,128)} %copy-done.16) | copy-start | bytes 9437188
  548.2 8.9 %copy-start.19 = (f32[1536,512]{1,0:T(8,128)S(1)}, f32[1536,512]{1,0:T(8,128)}, u32[]{:S(2)}) copy-start(f32[1536,512]{1,0:T(8,128)} %copy-done.18) | copy-start | bytes 9437188
  595.8 8.8 %copy-start.6 = (f32[16,128,128]{1,2,0:T(8,128)S(1)}, f32[16,128,128]{1,2,0:T(8,128)}, u32[]{:S(2)}) copy-start(f32[16,128,128]{1,2,0:T(8,128)} %all-reduce.3.cloned.1.call-done) | copy-start | bytes 3145732
  604.6 76.6 %copy-start.9 = (bf16[128,2048]{1,0:T(8,128)(2,1)S(1)}, bf16[128,2048]{1,0:T(8,128)(2,1)}, u32[]{:S(2)}) copy-start(bf16[128,2048]{1,0:T(8,128)(2,1)} %param.11) | copy-start | bytes 1572868
  606.6 79.9 %copy-start.1 = (bf16[1,2048,512]{2,1,0:T(8,128)(2,1)S(1)}, bf16[1,2048,512]{2,1,0:T(8,128)(2,1)}, u32[]{:S(2)}) copy-start(bf16[1,2048,512]{2,1,0:T(8,128)(2,1)} %param.15) | copy-start | bytes 6291460
Sparse Core Ops, SparseCore 0:
  10.3 52.1 all-gather.4
  76.7 87.2 all-reduce.2
  548.3 41.5 all-gather.6
  595.9 85.2 all-reduce.4
where the time goes:
time: 702 us; the launch traced here: 693 us
  waiting for transfers between devices  321 us (46%)
  blocking collectives  149 us (21%)
  local copies, waits for them, and re-layouts  89.3 us (13%)
  matrix products  84.1 us (12%)
  other arithmetic  28.2 us (4%)
  between operations  14.6 us (2%)
    all_to_all x1, blocking collectives, side_by_side(): lax.all_to_all(both, axis, split_axis=split_dim, concat_axis=concat_dim,...  149 us
    all_to_all x1, waiting for transfers between devices, body(): lax.all_to_all(payload.astype(jnp.bfloat16), ('tm', 'expert'), split_axis...  99.8 us
    psum x1, waiting for transfers between devices, body(): lax.psum(inclusive_back.astype(jnp.bfloat16), 'expert').astype(jnp.float32)  73.6 us
    psum x1, waiting for transfers between devices, body(): states = lax.psum(inclusive, 'expert')  70.4 us
    all_gather x1, waiting for transfers between devices, body(): everyone = lax.all_gather(local[None], 'tm', axis=0, tiled=True)  52.6 us
    all_gather x1, waiting for transfers between devices, body(): lax.all_gather(local_back[None].astype(jnp.bfloat16), 'tm', axis=0, tiled...  24.5 us
  transfers between devices with their start and end apart: 5, of which 5 were waited for; matrix products, arithmetic and copies ran while one was open for 7% of the time, Pallas kernels for 0%

commit v1 on v0

--- a/solution.py
+++ b/solution.py
@@ -8,6 +8,19 @@
 SLICES = 4
 epsilon = 1e-06
 highest = lax.Precision.HIGHEST
+
+
+def gather_around(shard, axis, dim):
+    ways = lax.axis_size(axis)
+    up = [(d, (d + 1) % ways) for d in range(ways)]
+    down = [(d, (d - 1) % ways) for d in range(ways)]
+    earlier, later = ([shard], [shard])
+    for _ in range(ways // 2):
+        earlier.append(lax.ppermute(earlier[-1], axis, up))
+    for _ in range((ways - 1) // 2):
+        later.append(lax.ppermute(later[-1], axis, down))
+    line = jnp.concatenate([*earlier[::-1], *later[1:]], axis=dim)
+    return jnp.roll(line, (lax.axis_index(axis) - ways // 2) * shard.shape[dim], axis=dim)
 
 
 def side_by_side(arrays, axis, split_dim, concat_dim, along):
@@ -100,9 +113,7 @@
     )
     query_grad = jnp.einsum("thb,hab->tha", norm_grad, states, precision=highest)
     local_back = jnp.einsum("tha,thb->hab", query_f, norm_grad, precision=highest)
-    every_back = lax.all_gather(
-        local_back[None].astype(jnp.bfloat16), "tm", axis=0, tiled=True
-    ).astype(jnp.float32)
+    every_back = gather_around(local_back[None].astype(jnp.bfloat16), "tm", 0).astype(jnp.float32)
     mine_back = lax.axis_index("tm")
     picks_back = (jnp.arange(every_back.shape[0], dtype=jnp.int32) >= mine_back).astype(jnp.float32)
     inclusive_back = jnp.einsum("c,chab->hab", picks_back, every_back, precision=highest)

time: 702 us -> 726 us (1.034)
  local copies, waits for them, and re-layouts: 89.3 us -> 101 us
  starting transfers between devices: 7.02 us -> 15.9 us
    all_gather x1 -> x0, waiting for transfers between devices: 24.5 us -> none  [body(): lax.all_gather(local_back[None].astype(jnp.bfloat16), 'tm', axis=0, tiled...]
    ppermute x0 -> x7, waiting for transfers between devices: none -> 21.9 us  [the longest x4 16.8 us: gather_around(): earlier.append(lax.ppermute(earlier[-1], axis, up))]
    dynamic_slice x0 -> x2, local copies, waits for them, and re-layouts: none -> 9.05 us  [gather_around(): jnp.roll(line, (lax.axis_index(axis) - ways // 2) * shard.shape[dim], axi...]
    ppermute x0 -> x7, starting transfers between devices: none -> 8.87 us  [the longest x3 8.84 us: gather_around(): later.append(lax.ppermute(later[-1], axis, down))]
  transfers between devices with their start and end apart: 5 -> 11, of which waited for: 5 -> 7; matrix products, arithmetic and copies ran while one was open for 7% -> 7% of each run, Pallas kernels for 0% -> 0%
where the time goes in v1:
time: 726 us; the launch traced here: 717 us
  waiting for transfers between devices  323 us (44%)
  blocking collectives  149 us (21%)
  local copies, waits for them, and re-layouts  101 us (14%)
  matrix products  85 us (12%)
  other arithmetic  29.2 us (4%)
  starting transfers between devices  15.9 us (2%)
  between operations  14.7 us (2%)
    all_to_all x1, blocking collectives, side_by_side(): lax.all_to_all(both, axis, split_axis=split_dim, concat_axis=concat_dim,...  149 us
    all_to_all x1, waiting for transfers between devices, body(): lax.all_to_all(payload.astype(jnp.bfloat16), ('tm', 'expert'), split_axis...  99.8 us
    psum x1, waiting for transfers between devices, body(): lax.psum(inclusive_back.astype(jnp.bfloat16), 'expert').astype(jnp.float32)  77.8 us
    psum x1, waiting for transfers between devices, body(): states = lax.psum(inclusive, 'expert')  70.4 us
    all_gather x1, waiting for transfers between devices, body(): everyone = lax.all_gather(local[None], 'tm', axis=0, tiled=True)  52.6 us
    ppermute x4, waiting for transfers between devices, gather_around(): earlier.append(lax.ppermute(earlier[-1], axis, up))  16.8 us
  transfers between devices with their start and end apart: 11, of which 7 were waited for; matrix products, arithmetic and copies ran while one was open for 7% of the time, Pallas kernels for 0%

profile of v1, /device:TPU:0, one launch (start us, length us, event | category | flops | bytes accessed | tf_op | source)
XLA Modules:
  0.0 717.3 jit_solution(351277335510657424)
XLA Ops:
  7.2 2.7 fusion.21
  10.0 52.6 %all-gather.3.cloned.1.call-done = f32[128,128,128]{2,1,0:T(8,128)} async-done(((f32[16,128,128]{2,1,0:T(8,128)}), f32[128,128,128]{2,1,0:T(8,128)}) %all-gather.3.cloned.1.call-update) | async-done | bytes 8388624 | tf_op jit(solution)/shard_map/all_gather | solution.py:72
  62.5 11.9 %fusion = f32[1,16,128,128]{3,0,2,1:T(1,128)S(1)} fusion(f32[8,16,128,128]{3,2,1,0:T(8,128)} %bitcast.138, s32[]{:T(128)S(6)} %axis_index.11), kind=kOutput, calls=%fused_computation.6 | convolution fusion | flops 25165832 | bytes 9437188 | tf_op jit(solution)/shard_map/c,chab->hab/dot_general | solution.py:75
  74.4 2.1 copy.70
  77.0 0.6 reduce-window.6
  77.6 0.2 slice_reduce_fusion
  78.2 3.4 broadcast_in_dim.52
  81.6 3.6 reshape.151
  85.4 4.5 scatter_custom_fusion.1
  89.9 3.6 reshape.152
  93.5 70.4 %all-reduce.3.cloned.1.call-done = f32[16,128,128]{1,2,0:T(8,128)} async-done(((f32[16,128,128]{1,2,0:T(8,128)}), f32[16,128,128]{1,2,0:T(8,128)}) %all-reduce.3.cloned.1.call-update) | async-done | bytes 1048592 | tf_op jit(solution)/shard_map/psum | solution.py:76
  164.0 2.4 multiply_reduce_fusion.1
  166.4 1.0 copy-done.2
  167.5 1.0 copy.56
  168.6 1.7 broadcast_in_dim.50
  170.2 1.2 reshape.172
  171.5 4.1 scatter_custom_fusion
  175.6 3.6 reshape.149
  179.2 6.1 broadcast_in_dim.53
  185.2 4.3 broadcast_in_dim.51
  189.5 9.2 %pad_maximum_fusion = bf16[128,24,2048]{2,1,0:T(8,128)(2,1)S(1)} fusion(bf16[128,12,2048]{2,1,0:T(8,128)(2,1)} %bitcast.134, bf16[128,12,2048]{2,1,0:T(8,128)(2,1)} %bitcast.135), kind=kLoop, calls=%fused_computation.4 | loop fusion | flops 25165824 | bytes 25165824 | tf_op jit(solution)/shard_map/concatenate | solution.py:28
  198.7 149.1 %all_to_all.10 = bf16[128,24,2048]{2,1,0:T(8,128)(2,1)S(1)} all-to-all(bf16[128,24,2048]{2,1,0:T(8,128)(2,1)S(1)} %pad_maximum_fusion), channel_id=1, replica_groups=mesh['tm'=8,'expert'=16] {'tm','expert'}, dimensions={0} | all-to-all | bytes 25165824 | tf_op jit(solution)/shard_map/all_to_all | solution.py:29
  347.9 7.1 fusion.45
  355.0 10.7 %reshape_reshape.6 = bf16[1536,2048]{1,0:T(8,128)(2,1)} reshape(bf16[128,12,2048]{2,1,0:T(8,128)(2,1)} %get-tuple-element.24) | data formatting | bytes 12582912 | tf_op jit(solution)/shard_map/reshape;reshape | solution.py:97
  365.7 10.7 %reshape_reshape.7 = bf16[1536,2048]{1,0:T(8,128)(2,1)} reshape(bf16[128,12,2048]{2,1,0:T(8,128)(2,1)} %get-tuple-element.25) | data formatting | bytes 12582912 | tf_op jit(solution)/shard_map/reshape;reshape | solution.py:96
  376.4 5.9 fusion.4
  382.4 3.4 fusion.7
  385.9 4.8 multiply_convert_fusion.1
  390.8 6.5 fusion.2
  397.3 8.5 %add_convert_fusion = bf16[1536,2048]{1,0:T(8,128)(2,1)} fusion(f32[1536,2048]{1,0:T(8,128)} %fusion.2, bf16[1536,512]{1,0:T(8,128)(2,1)S(1)} %get-tuple-element.26, bf16[1,2048,512]{2,1,0:T(8,128)(2,1)S(1)} %copy-done.13), kind=kOutput, calls=%fused_computation.5 | convolution fusion | flops 3227516928 | bytes 22544384 | tf_op jit(solution)/shard_map/dot_general | solution.py:53
  405.8 10.6 %convert_element_type.88 = bf16[128,12,2048]{2,1,0:T(8,128)(2,1)} reshape(bf16[1536,2048]{1,0:T(8,128)(2,1)} %add_convert_fusion) | data formatting | bytes 12582912 | tf_op jit(solution)/shard_map/convert_element_type | solution.py:103
  416.4 6.9 all-to-all-start.1
  423.5 99.8 %all-to-all-done.1 = bf16[128,12,2048]{2,1,0:T(8,128)(2,1)} async-done(((bf16[128,12,2048]{2,1,0:T(8,128)(2,1)}), bf16[128,12,2048]{2,1,0:T(8,128)(2,1)}, u32[]{:S(2)}, u32[]{:S(2)}) %all-to-all-start.1) | async-done | bytes 6291488 | tf_op jit(solution)/shard_map/all_to_all | solution.py:102
  523.3 7.8 %convert_reduce_fusion = f32[32,12,2048]{2,1,0:T(8,128)} fusion(bf16[128,12,2048]{2,1,0:T(8,128)(2,1)} %all-to-all-done.1), kind=kLoop, calls=%fused_computation.3 | loop fusion | flops 5505024 | bytes 9437184 | tf_op jit(solution)/shard_map/reduce_sum | solution.py:105
  531.2 3.0 reshape.156
  534.2 2.7 gather_fusion
  536.9 2.5 gather.7
  539.4 4.5 select_reduce_fusion
  543.9 1.2 convert_add_fusion
  545.0 0.3 copy.58
  545.4 0.2 multiply_reduce_fusion
  545.6 2.0 fusion.12
  547.6 9.8 %collective-permute-done = bf16[1,16,128,128]{2,3,1,0:T(8,128)(2,1)S(1)} collective-permute-done((bf16[1,16,128,128]{2,3,1,0:T(8,128)(2,1)S(1)}, bf16[1,16,128,128]{2,3,1,0:T(8,128)(2,1)S(1)}, u32[]{:S(2)}, u32[]{:S(2)}) %collective-permute-start) | collective-permute-done | bytes 524320 | tf_op jit(solution)/shard_map/ppermute | solution.py:19
  557.4 3.0 collective-permute-start.4
  560.4 7.0 collective-permute-done.1
  567.3 10.3 %convolution_bitcast_fusion = f32[1,512,2048]{2,1,0:T(8,128)} fusion(bf16[1536,2048]{1,0:T(8,128)(2,1)} %reshape_reshape.6, f32[1536,512]{1,0:T(8,128)} %copy-done.18, f32[1536,512]{1,0:T(8,128)} %copy-done.17), kind=kOutput, calls=%fused_computation.8 | convolution fusion | flops 3225944064 | bytes 16777216 | tf_op jit(solution)/shard_map/dot_general | solution.py:47
  577.6 3.0 collective-permute-start.5
  580.6 8.2 %convolution_bitcast_fusion.1 = f32[1,2048,512]{2,1,0:T(8,128)} fusion(bf16[1536,2048]{1,0:T(8,128)(2,1)} %reshape_reshape.7, bf16[1536,512]{1,0:T(8,128)(2,1)S(1)} %copy-done.15), kind=kOutput, calls=%fused_computation.9 | convolution fusion | flops 3221225472 | bytes 12058624 | tf_op jit(solution)/shard_map/dot_general | solution.py:51
  588.8 2.9 collective-permute-start.6
  591.8 1.1 constant_dynamic-update-slice_fusion.13
  593.2 5.1 collective-permute-done.6
  598.6 1.1 constant_dynamic-update-slice_fusion.5
  600.1 2.3 constant_dynamic-slice_fusion
  602.5 6.7 copy.74
  609.2 3.4 fusion.35
  612.6 0.9 convert_element_type.95
  613.5 8.9 %convolution_bitcast_fusion.2 = f32[1,2048,512]{2,1,0:T(8,128)} fusion(bf16[1536,2048]{1,0:T(8,128)(2,1)} %reshape_reshape.7, bf16[1536,512]{1,0:T(8,128)(2,1)} %copy-done.16), kind=kOutput, calls=%fused_computation.10 | convolution fusion | flops 3221225472 | bytes 12058624 | tf_op jit(solution)/shard_map/dot_general | solution.py:50
  622.4 2.8 convolution_convert_fusion.3
  625.2 2.0 copy.65
  627.2 77.8 %all-reduce.5.cloned.1.call-done = bf16[16,128,128]{2,1,0:T(8,128)(2,1)} async-done(((bf16[16,128,128]{2,1,0:T(8,128)(2,1)}), bf16[16,128,128]{2,1,0:T(8,128)(2,1)}) %all-reduce.5.cloned.1.call-update) | async-done | bytes 524304 | tf_op jit(solution)/shard_map/psum | solution.py:120
  705.0 1.7 convolution_convert_fusion.1
  706.7 1.0 copy.66
  707.7 1.7 convolution_convert_fusion
  709.4 1.0 copy.67
  (88 shorter events, 2.5 us)
Async XLA Ops:
  7.2 369.2 %copy-start = (bf16[1,2048,512]{2,1,0:T(8,128)(2,1)S(1)}, bf16[1,2048,512]{2,1,0:T(8,128)(2,1)}, u32[]{:S(2)}) copy-start(bf16[1,2048,512]{2,1,0:T(8,128)(2,1)} %param.15) | copy-start | bytes 6291460
  7.2 55.4 %all-gather.3.cloned.1.call-start = ((), (), s32[]{:S(2)}) async-start(), calls=%async_computation.4 | async-start | bytes 9437184 | tf_op jit(solution)/shard_map/all_gather | solution.py:72
  9.9 154.1 %all-reduce.3.cloned.1.call-start = ((), (), s32[]{:S(2)}) async-start(), calls=%async_computation.2 | async-start | bytes 2097152 | tf_op jit(solution)/shard_map/psum | solution.py:76
  62.5 14.0 %copy-start.10 = (s32[128,2]{0,1:T(2,128)S(1)}, s32[128,2]{0,1:T(2,128)}, u32[]{:S(2)}) copy-start(s32[128,2]{0,1:T(2,128)} %param.13) | copy-start | bytes 3076
  62.5 15.4 %copy-start.11 = (f32[128,2]{0,1:T(2,128)S(1)}, f32[128,2]{0,1:T(2,128)}, u32[]{:S(2)}) copy-start(f32[128,2]{0,1:T(2,128)} %param.14) | copy-start | bytes 3076
  85.3 78.7 %copy-start.9 = (bf16[128,2048]{1,0:T(8,128)(2,1)S(1)}, bf16[128,2048]{1,0:T(8,128)(2,1)}, u32[]{:S(2)}) copy-start(bf16[128,2048]{1,0:T(8,128)(2,1)} %param.9) | copy-start | bytes 1572868
  166.4 1.0 copy-start.2
  179.2 6.1 copy-start.6
  376.4 6.0 copy-start.7
  376.4 6.0 copy-start.13
  376.4 9.5 %slice-start = ((s8[6291456]{0:T(1024)(128)(4,1)}), s8[4194304]{0:T(1024)(128)(4,1)S(1)}, s32[]{:S(2)}) async-start(s8[6291456]{0:T(1024)(128)(4,1)} %bitcast.139), calls=%async_computation.5 | async-start | bytes 8388608
  382.4 3.5 copy-start.17
  382.4 3.5 slice-start.1
  382.4 3.5 copy-start.12
  385.9 4.9 copy-start.18
  390.8 6.5 copy-start.16
  390.8 6.5 copy-start.14
  416.4 106.9 %all-to-all-start.1 = ((bf16[128,12,2048]{2,1,0:T(8,128)(2,1)}), bf16[128,12,2048]{2,1,0:T(8,128)(2,1)}, u32[]{:S(2)}, u32[]{:S(2)}) async-start(bf16[128,12,2048]{2,1,0:T(8,128)(2,1)} %convert_element_type.88), calls=%async_computation.1 | async-start | bytes 16777216 | tf_op jit(solution)/shard_map/all_to_all | solution.py:102
  423.3 281.7 %all-reduce.5.cloned.1.call-start = ((), (), s32[]{:S(2)}) async-start(), calls=%async_computation.3 | async-start | bytes 1048576 | tf_op jit(solution)/shard_map/psum | solution.py:120
  539.4 6.0 copy-start.3
  545.4 32.2 %copy-start.4 = (f32[128,2048]{0,1:T(8,128)}, f32[128,2048]{0,1:T(8,128)S(1)}, u32[]{:S(2)}) copy-start(f32[128,2048]{0,1:T(8,128)S(1)} %copy.58) | copy-start | bytes 3145732
  547.6 9.8 %collective-permute-start = (bf16[1,16,128,128]{2,3,1,0:T(8,128)(2,1)S(1)}, bf16[1,16,128,128]{2,3,1,0:T(8,128)(2,1)S(1)}, u32[]{:S(2)}, u32[]{:S(2)}) collective-permute-start(bf16[1,16,128,128]{2,3,1,0:T(8,128)(2,1)S(1)} %fusion.12), channel_id=1, source_target_pairs={{0,16},{16,32},{32,48},{48,64},{64,80},{80,96},{96,112},{112,0},{1... | collective-permute-start | bytes 1572872 | tf_op jit(solution)/shard_map/ppermute | solution.py:19
  557.4 9.9 %collective-permute-start.1 = (bf16[1,16,128,128]{2,3,1,0:T(8,128)(2,1)S(1)}, bf16[1,16,128,128]{2,3,1,0:T(8,128)(2,1)}, u32[]{:S(2)}, u32[]{:S(2)}) collective-permute-start(bf16[1,16,128,128]{2,3,1,0:T(8,128)(2,1)S(1)} %collective-permute-done), channel_id=1, source_target_pairs={{0,16},{16,32},{32,48},{48,64},{64,80},{80,96},{96,112},{112,0},{1... | collective-permute-start | bytes 1572872 | tf_op jit(solution)/shard_map/ppermute | solution.py:19
  557.4 23.2 %copy-start.15 = (bf16[1536,512]{1,0:T(8,128)(2,1)S(1)}, bf16[1536,512]{1,0:T(8,128)(2,1)}, u32[]{:S(2)}) copy-start(bf16[1536,512]{1,0:T(8,128)(2,1)} %copy-done.14) | copy-start | bytes 4718596
  557.4 20.2 %collective-permute-start.4 = (bf16[1,16,128,128]{2,3,1,0:T(8,128)(2,1)S(1)}, bf16[1,16,128,128]{2,3,1,0:T(8,128)(2,1)S(1)}, u32[]{:S(2)}, u32[]{:S(2)}) collective-permute-start(bf16[1,16,128,128]{2,3,1,0:T(8,128)(2,1)S(1)} %fusion.12), channel_id=1, source_target_pairs={{0,112},{16,0},{32,16},{48,32},{64,48},{80,64},{96,80},{112,96},{1... | collective-permute-start | bytes 1572872 | tf_op jit(solution)/shard_map/ppermute | solution.py:21
  567.3 13.2 %collective-permute-start.2 = (bf16[1,16,128,128]{2,3,1,0:T(8,128)(2,1)}, bf16[1,16,128,128]{2,3,1,0:T(8,128)(2,1)S(1)}, u32[]{:S(2)}, u32[]{:S(2)}) collective-permute-start(bf16[1,16,128,128]{2,3,1,0:T(8,128)(2,1)} %collective-permute-done.1), channel_id=1, source_target_pairs={{0,16},{16,32},{32,48},{48,64},{64,80},{80,96},{96,112},{112,0},{1... | collective-permute-start | bytes 1572872 | tf_op jit(solution)/shard_map/ppermute | solution.py:19
  577.6 11.1 %collective-permute-start.5 = (bf16[1,16,128,128]{2,3,1,0:T(8,128)(2,1)S(1)}, bf16[1,16,128,128]{2,3,1,0:T(8,128)(2,1)S(1)}, u32[]{:S(2)}, u32[]{:S(2)}) collective-permute-start(bf16[1,16,128,128]{2,3,1,0:T(8,128)(2,1)S(1)} %collective-permute-done.4), channel_id=1, source_target_pairs={{0,112},{16,0},{32,16},{48,32},{64,48},{80,64},{96,80},{112,96},{1... | collective-permute-start | bytes 1572872 | tf_op jit(solution)/shard_map/ppermute | solution.py:21
  580.6 11.1 %collective-permute-start.3 = (bf16[1,16,128,128]{2,3,1,0:T(8,128)(2,1)S(1)}, bf16[1,16,128,128]{2,3,1,0:T(8,128)(2,1)S(1)}, u32[]{:S(2)}, u32[]{:S(2)}) collective-permute-start(bf16[1,16,128,128]{2,3,1,0:T(8,128)(2,1)S(1)} %collective-permute-done.2), channel_id=1, source_target_pairs={{0,16},{16,32},{32,48},{48,64},{64,80},{80,96},{96,112},{112,0},{1... | collective-permute-start | bytes 1572872 | tf_op jit(solution)/shard_map/ppermute | solution.py:19
  588.8 9.6 %collective-permute-start.6 = (bf16[1,16,128,128]{2,3,1,0:T(8,128)(2,1)S(1)}, bf16[1,16,128,128]{2,3,1,0:T(8,128)(2,1)S(1)}, u32[]{:S(2)}, u32[]{:S(2)}) collective-permute-start(bf16[1,16,128,128]{2,3,1,0:T(8,128)(2,1)S(1)} %collective-permute-done.5), channel_id=1, source_target_pairs={{0,112},{16,0},{32,16},{48,32},{64,48},{80,64},{96,80},{112,96},{1... | collective-permute-start | bytes 1572872 | tf_op jit(solution)/shard_map/ppermute | solution.py:21
  613.5 8.9 %copy-start.5 = (f32[128,2048]{0,1:T(8,128)S(1)}, f32[128,2048]{0,1:T(8,128)}, u32[]{:S(2)}) copy-start(f32[128,2048]{0,1:T(8,128)} %copy-done.4) | copy-start | bytes 3145732
  613.5 8.9 %copy-start.8 = (f32[16,128,128]{1,2,0:T(8,128)S(1)}, f32[16,128,128]{1,2,0:T(8,128)}, u32[]{:S(2)}) copy-start(f32[16,128,128]{1,2,0:T(8,128)} %all-reduce.3.cloned.1.call-done) | copy-start | bytes 3145732
  613.5 96.9 %copy-start.1 = (bf16[1,2048,512]{2,1,0:T(8,128)(2,1)S(1)}, bf16[1,2048,512]{2,1,0:T(8,128)(2,1)}, u32[]{:S(2)}) copy-start(bf16[1,2048,512]{2,1,0:T(8,128)(2,1)} %param.15) | copy-start | bytes 6291460
Sparse Core Ops, SparseCore 0:
  10.3 52.1 all-gather.2
  76.7 87.2 all-reduce.2
  613.6 91.3 all-reduce.4
